TPU v7x, 512 devices: a whole 4x8x8 slice. The times are simulated.
512 devices in a mesh: win: 16 (over y_lo, z), seq: 4 (over y_hi), chan: 8 (over x, core).
Axes of the slice: x: 4, y: 8 (y_hi: 4, y_lo: 2; y = y_hi * 2 + y_lo), z: 8, core: 2. Of those that a mesh axis runs over, the one named last changes fastest.
Arguments:
- first_gate_1: bfloat16 [16, 1024, 4096], P('win', 'seq', 'chan'), may hold values from -6 to 6
- operator_values: bfloat16 [16, 1024, 4096], P('win', 'seq', 'chan'), may hold values from -6 to 6
- second_gate_2: bfloat16 [16, 1024, 4096], P('win', 'seq', 'chan'), may hold values from -6 to 6
- convolved_output: bfloat16 [16, 1024, 4096], P('win', 'seq', 'chan'), may hold values from -6 to 6
- output_gradient: bfloat16 [16, 1024, 4096], P('win', 'seq', 'chan'), may hold values from -6 to 6
- frozen_gradient: bfloat16 [16, 1024, 4096], P('win', 'seq', 'chan'), may hold values from -6 to 6
- filt: bfloat16 [1024, 4096], P('seq', 'chan'), may hold values from -1 to 1
- adapter_down_weight: bfloat16 [4096, 64], P('chan'), may hold values from -0.09375 to 0.09375
- adapter_up_weight: bfloat16 [64, 4096], P(None, 'chan'), may hold values from -0.09375 to 0.09375
Outputs:
- grad_x1: bfloat16 [16, 1024, 4096], P('win', 'seq', 'chan')
- grad_values: bfloat16 [16, 1024, 4096], P('win', 'seq', 'chan')
- grad_x2: bfloat16 [16, 1024, 4096], P('win', 'seq', 'chan')
- grad_a: float32 [4096, 64], P('chan')
- grad_b: float32 [64, 4096], P(None, 'chan')
All inputs are finite; a program needn't handle non-finite values.
Results may differ from a plain program's by a relative error of at most 0.005.
Values may be sent and summed in bfloat16 or wider, within the bound.
A program may use at most 64 MiB of HBM per device.

v0:
```python
import math

import jax
import jax.numpy as jnp
from jax import lax
from jax.sharding import PartitionSpec as P

adapter_scaling = 2.0
highest = lax.Precision.HIGHEST


def passed_along(value, axis, by):
    peers = lax.axis_size(axis)
    pairs = [(i, i + by) for i in range(peers) if 0 <= i + by < peers]
    return lax.ppermute(value, axis, pairs)


def fourier_table(rows):
    period = 2 * rows
    freq = lax.broadcasted_iota(jnp.int32, (period, rows), 0)
    place = lax.broadcasted_iota(jnp.int32, (period, rows), 1)
    angle = 2.0 * math.pi / period * (freq * place % period).astype(jnp.float32)
    return jnp.concatenate([jnp.cos(angle), -jnp.sin(angle)], axis=0)


def transform(table, block):
    return jnp.einsum(
        "ft,wtc->wfc", table, block, precision=highest, preferred_element_type=jnp.float32
    )


def correlate(spectrum, filter_spec):
    half = filter_spec.shape[0] // 2
    real_d, imag_d = (spectrum[:, :half], spectrum[:, half:])
    real_g, imag_g = (filter_spec[:half], filter_spec[half:])
    return jnp.concatenate(
        [real_d * real_g + imag_d * imag_g, imag_d * real_g - real_d * imag_g], axis=1
    )


def on_device(
    first_gate_1,
    operator_values,
    second_gate_2,
    convolved_output,
    output_gradient,
    frozen_gradient,
    filt,
    adapter_down_weight,
    adapter_up_weight,
):
    wins, rows, chans = first_gate_1.shape
    blocks = lax.axis_size("seq")
    table = fourier_table(rows)
    width = 4 * rows
    gated_output = (
        second_gate_2.astype(jnp.float32) * convolved_output.astype(jnp.float32)
    ).astype(jnp.bfloat16)
    input_piece = jnp.einsum(
        "ofe,ey->ofy", gated_output, adapter_down_weight, preferred_element_type=jnp.float32
    )
    backward_piece = jnp.einsum(
        "izj,hj->izh", output_gradient, adapter_up_weight, preferred_element_type=jnp.float32
    )
    lowrank_input, lowrank_backward = lax.psum((input_piece, backward_piece), "chan")
    lowrank_input = lowrank_input.astype(jnp.bfloat16)
    lowrank_backward = lowrank_backward.astype(jnp.bfloat16)
    gated_gradient = frozen_gradient.astype(jnp.float32) + adapter_scaling * jnp.einsum(
        "vds,fs->vdf", lowrank_backward, adapter_down_weight, preferred_element_type=jnp.float32
    )
    grad_x2 = (gated_gradient * convolved_output.astype(jnp.float32)).astype(jnp.bfloat16)
    grad_conv = gated_gradient * second_gate_2.astype(jnp.float32)
    factor = adapter_scaling / math.sqrt(wins * lax.axis_size("win") * rows * blocks)
    part_a = factor * jnp.einsum(
        "wtc,wtr->cr", gated_output, lowrank_backward, preferred_element_type=jnp.float32
    )
    part_b = factor * jnp.einsum(
        "wtr,wtc->rc", lowrank_input, output_gradient, preferred_element_type=jnp.float32
    )
    grad_a, grad_b = lax.psum((part_a, part_b), ("win", "seq"))
    carry = jnp.zeros((blocks, width, chans), jnp.float32)
    piece = lax.all_gather(filt, "seq", axis=0, tiled=True)
    for inner in range(piece.shape[0] // rows):
        block = piece[inner * rows : (inner + 1) * rows].astype(jnp.float32)
        spec = jnp.dot(table, block, precision=highest, preferred_element_type=jnp.float32)
        carry = lax.dynamic_update_index_in_dim(carry, spec, inner, 0)
    parity = lax.broadcasted_iota(jnp.int32, (width, 1), 0) % (2 * rows) % 2
    flips = (1 - 2 * parity).astype(jnp.float32)
    shifted = [carry[0]]
    for lag in range(1, blocks):
        shifted.append(carry[lag] + flips * carry[lag - 1])
    filter_specs = jnp.stack(shifted, axis=0)
    total = jnp.zeros((wins, width, chans), jnp.float32)
    current = grad_conv
    for lag in range(blocks):
        if lag > 0:
            current = passed_along(current, "seq", -1)
        total = total + correlate(transform(table, current), filter_specs[lag])
    grad_mixed = jnp.einsum(
        "fj,wfc->wjc", table, total, precision=highest, preferred_element_type=jnp.float32
    ) / (2.0 * rows)
    grad_x1 = (grad_mixed * operator_values.astype(jnp.float32)).astype(jnp.bfloat16)
    grad_values = (grad_mixed * first_gate_1.astype(jnp.float32)).astype(jnp.bfloat16)
    return (grad_x1, grad_values, grad_x2, grad_a, grad_b)


def solution(mesh):
    in_specs = (
        P("win", "seq", "chan"),
        P("win", "seq", "chan"),
        P("win", "seq", "chan"),
        P("win", "seq", "chan"),
        P("win", "seq", "chan"),
        P("win", "seq", "chan"),
        P("seq", "chan"),
        P("chan", None),
        P(None, "chan"),
    )
    out_specs = (
        P("win", "seq", "chan"),
        P("win", "seq", "chan"),
        P("win", "seq", "chan"),
        P("chan", None),
        P(None, "chan"),
    )
    return jax.shard_map(
        on_device, mesh=mesh, in_specs=in_specs, out_specs=out_specs, check_vma=False
    )
```

profile of v0, /device:TPU:1, one launch (start us, length us, event | category | flops | bytes accessed | tf_op | source)
XLA Modules:
  0.0 262.8 jit_solution(9713839780466887257)
XLA Ops:
  8.0 0.0 copy-start
  8.0 0.0 copy-start.5
  8.0 0.0 copy-start.4
  8.0 0.0 all-gather.2.cloned.1.call-start
  8.1 0.7 all-gather.2.cloned.1.call-update
  8.8 0.0 all-reduce.5.cloned.1.call-start
  8.8 1.2 convolution_bitcast_fusion.4
  10.1 1.0 convolution_bitcast_fusion.5
  11.1 28.9 %all-reduce.6 = (bf16[1,256,64]{1,2,0:T(8,128)(2,1)S(1)}, bf16[1,256,64]{1,2,0:T(8,128)(2,1)S(1)}) all-reduce(f32[1,256,64]{1,2,0:T(8,128)S(1)} %convolution_bitcast_fusion.5, f32[1,256,64]{1,2,0:T(8,128)S(1)} %convolution_bitcast_fusion.4), channel_id=1, replica_groups=mesh['win'=16,'seq'=4,'chan'=8] {'chan'}, use_global_device_ids=true, to_apply=%region_0.1 | all-reduce | flops 32768 | bytes 196608 | tf_op jit(solution)/shard_map/psum | solution.py:65
  40.1 2.2 fusion.23
  42.3 0.8 copy-done.6
  43.1 1.3 collective-permute-start
  44.4 42.0 %collective-permute-done = f32[1,256,512]{2,1,0:T(8,128)S(1)} collective-permute-done((f32[1,256,512]{2,1,0:T(8,128)S(1)}, f32[1,256,512]{2,1,0:T(8,128)S(1)}, u32[]{:S(2)}, u32[]{:S(2)}) %collective-permute-start) | collective-permute-done | bytes 524320 | tf_op jit(solution)/shard_map/ppermute | solution.py:15
  86.3 1.3 collective-permute-start.1
  87.6 0.8 convolution_multiply_fusion.2
  88.5 0.9 convolution_multiply_fusion.1
  89.3 0.0 all-reduce.5.cloned.1.call-update
  89.4 2.1 sine_negate_fusion
  91.4 21.7 %collective-permute-done.1 = f32[1,256,512]{2,1,0:T(8,128)} collective-permute-done((f32[1,256,512]{2,1,0:T(8,128)S(1)}, f32[1,256,512]{2,1,0:T(8,128)}, u32[]{:S(2)}, u32[]{:S(2)}) %collective-permute-start.1) | collective-permute-done | bytes 524320 | tf_op jit(solution)/shard_map/ppermute | solution.py:15
  113.1 1.5 collective-permute-start.2
  114.6 0.8 copy.21
  115.5 0.8 copy.22
  116.3 4.6 %convolution_bitcast_fusion.3 = f32[1,1024,512]{1,2,0:T(8,128)S(1)} fusion(f32[1,256,512]{2,1,0:T(8,128)} %copy-done.6, f32[512,256]{1,0:T(8,128)S(1)} %get-tuple-element.29, f32[512,256]{1,0:T(8,128)S(1)} %get-tuple-element.30), kind=kOutput, calls=%fused_computation.21 | convolution fusion | flops 1610874880 | bytes 3670016 | tf_op jit(solution)/shard_map/ft,wtc->wfc/dot_general | solution.py:27
  120.9 4.8 %convolution_bitcast_fusion.2 = f32[1,1024,512]{1,2,0:T(8,128)} fusion(f32[1,256,512]{2,1,0:T(8,128)S(1)} %copy-done.11, f32[512,256]{1,0:T(8,128)S(1)} %get-tuple-element.29, f32[512,256]{1,0:T(8,128)S(1)} %get-tuple-element.30), kind=kOutput, calls=%fused_computation.20 | convolution fusion | flops 1610874880 | bytes 3670016 | tf_op jit(solution)/shard_map/ft,wtc->wfc/dot_general | solution.py:27
  125.7 5.8 %convolution_bitcast_fusion.1 = f32[1,1024,512]{1,2,0:T(8,128)} fusion(f32[1,256,512]{2,1,0:T(8,128)} %collective-permute-done.1, f32[512,256]{1,0:T(8,128)S(1)} %get-tuple-element.29, f32[512,256]{1,0:T(8,128)S(1)} %get-tuple-element.30), kind=kOutput, calls=%fused_computation.19 | convolution fusion | flops 1610874880 | bytes 3670016 | tf_op jit(solution)/shard_map/ft,wtc->wfc/dot_general | solution.py:27
  131.5 0.1 collective-permute-done.2
  131.7 6.1 %convolution_bitcast_fusion = f32[1,1024,512]{1,2,0:T(8,128)} fusion(f32[1,256,512]{2,1,0:T(8,128)} %collective-permute-done.2, f32[512,256]{1,0:T(8,128)S(1)} %get-tuple-element.29, f32[512,256]{1,0:T(8,128)S(1)} %get-tuple-element.30), kind=kOutput, calls=%fused_computation.18 | convolution fusion | flops 1610874880 | bytes 3670016 | tf_op jit(solution)/shard_map/ft,wtc->wfc/dot_general | solution.py:27
  137.8 2.1 fusion.41
  139.9 1.1 fusion.39
  141.0 1.4 multiply_add_fusion.1
  142.5 1.2 multiply_add_fusion
  143.7 0.4 copy-done.3
  144.0 0.5 add_bitcast_fusion
  144.6 1.1 copy-done.2
  145.6 0.5 add_bitcast_fusion.1
  146.1 1.1 copy-done.1
  147.2 0.5 add_bitcast_fusion.2
  147.7 0.0 copy-start.7
  147.8 0.0 copy-start.8
  147.8 0.5 add_bitcast_fusion.3
  148.3 0.4 copy-done.7
  148.7 0.1 copy-done.8
  148.8 2.0 multiply_convert_fusion
  150.8 0.8 copy.23
  151.6 0.8 copy.24
  152.4 99.7 %all-reduce.5.cloned.1.call-done = (f32[512,64]{0,1:T(8,128)}, f32[64,512]{1,0:T(8,128)}) async-done(((f32[512,64]{0,1:T(8,128)}, f32[64,512]{1,0:T(8,128)}), (f32[512,64]{0,1:T(8,128)}, f32[64,512]{1,0:T(8,128)})) %all-reduce.5.cloned.1.call-update) | async-done | bytes 262160 | tf_op jit(solution)/shard_map/psum | solution.py:80
  252.2 1.6 copy.35
  253.8 1.6 copy.36
  (19 shorter events, 0.0 us)
Async XLA Ops:
  8.0 2.1 copy-start
  8.0 80.5 %copy-start.5 = (bf16[1,256,512]{2,1,0:T(8,128)(2,1)S(1)}, bf16[1,256,512]{2,1,0:T(8,128)(2,1)}, u32[]{:S(2)}) copy-start(bf16[1,256,512]{2,1,0:T(8,128)(2,1)} %param.11) | copy-start | bytes 786436
  8.0 80.4 %copy-start.4 = (bf16[1,256,512]{2,1,0:T(8,128)(2,1)S(1)}, bf16[1,256,512]{2,1,0:T(8,128)(2,1)}, u32[]{:S(2)}) copy-start(bf16[1,256,512]{2,1,0:T(8,128)(2,1)} %param.12) | copy-start | bytes 786436
  8.0 129.7 %all-gather.2.cloned.1.call-start = ((), (), s32[]{:S(2)}) async-start(), calls=%async_computation | async-start | bytes 1310720 | tf_op jit(solution)/shard_map/all_gather | solution.py:82
  8.8 243.4 %all-reduce.5.cloned.1.call-start = ((), (), s32[]{:S(2)}) async-start(), calls=%async_computation.1 | async-start | bytes 524288 | tf_op jit(solution)/shard_map/psum | solution.py:80
  11.1 103.5 %copy-start.12 = (bf16[1,256,512]{2,1,0:T(8,128)(2,1)S(1)}, bf16[1,256,512]{2,1,0:T(8,128)(2,1)}, u32[]{:S(2)}) copy-start(bf16[1,256,512]{2,1,0:T(8,128)(2,1)} %param.10) | copy-start | bytes 786436
  40.1 75.4 %copy-start.13 = (bf16[1,256,512]{2,1,0:T(8,128)(2,1)S(1)}, bf16[1,256,512]{2,1,0:T(8,128)(2,1)}, u32[]{:S(2)}) copy-start(bf16[1,256,512]{2,1,0:T(8,128)(2,1)} %param.9) | copy-start | bytes 786436
  42.3 0.8 copy-start.6
  43.1 43.3 %collective-permute-start = (f32[1,256,512]{2,1,0:T(8,128)S(1)}, f32[1,256,512]{2,1,0:T(8,128)S(1)}, u32[]{:S(2)}, u32[]{:S(2)}) collective-permute-start(f32[1,256,512]{2,1,0:T(8,128)S(1)} %get-tuple-element.25), channel_id=1, source_target_pairs={{8,0},{16,8},{24,16},{9,1},{17,9},{25,17},{10,2},{18,10},{26,18},{... | collective-permute-start | bytes 1572872 | tf_op jit(solution)/shard_map/ppermute | solution.py:15
  86.3 30.0 %copy-start.10 = (f32[1,256,512]{2,1,0:T(8,128)}, f32[1,256,512]{2,1,0:T(8,128)S(1)}, u32[]{:S(2)}) copy-start(f32[1,256,512]{2,1,0:T(8,128)S(1)} %collective-permute-done) | copy-start | bytes 1572868
  86.3 26.8 %collective-permute-start.1 = (f32[1,256,512]{2,1,0:T(8,128)S(1)}, f32[1,256,512]{2,1,0:T(8,128)}, u32[]{:S(2)}, u32[]{:S(2)}) collective-permute-start(f32[1,256,512]{2,1,0:T(8,128)S(1)} %collective-permute-done), channel_id=1, source_target_pairs={{8,0},{16,8},{24,16},{9,1},{17,9},{25,17},{10,2},{18,10},{26,18},{... | collective-permute-start | bytes 1572872 | tf_op jit(solution)/shard_map/ppermute | solution.py:15
  113.1 18.6 %collective-permute-start.2 = (f32[1,256,512]{2,1,0:T(8,128)}, f32[1,256,512]{2,1,0:T(8,128)}, u32[]{:S(2)}, u32[]{:S(2)}) collective-permute-start(f32[1,256,512]{2,1,0:T(8,128)} %collective-permute-done.1), channel_id=1, source_target_pairs={{8,0},{16,8},{24,16},{9,1},{17,9},{25,17},{10,2},{18,10},{26,18},{... | collective-permute-start | bytes 1572872 | tf_op jit(solution)/shard_map/ppermute | solution.py:15
  116.3 4.6 %copy-start.11 = (f32[1,256,512]{2,1,0:T(8,128)S(1)}, f32[1,256,512]{2,1,0:T(8,128)}, u32[]{:S(2)}) copy-start(f32[1,256,512]{2,1,0:T(8,128)} %copy-done.10) | copy-start | bytes 1572868
  137.8 2.1 copy-start.9
  142.5 1.6 copy-start.3
  144.0 1.6 copy-start.2
  145.6 1.6 copy-start.1
  147.7 1.0 copy-start.7
  147.8 1.0 copy-start.8
Sparse Core Ops, SparseCore 0:
  11.0 55.7 all-gather.1
Sparse Core Ops, SparseCore 1:
  89.4 162.7 all-reduce.4
where the time goes:
time: 267 us; the launch traced here: 263 us
  waiting for transfers between devices  164 us (61%)
  matrix products  35.3 us (13%)
  blocking collectives  28.9 us (11%)
  between operations  15.7 us (6%)
  local copies, waits for them, and re-layouts  10.4 us (4%)
  starting transfers between devices  4.1 us (2%)
  other arithmetic  4.09 us (2%)
    psum x1, waiting for transfers between devices, on_device(): grad_a, grad_b = lax.psum((part_a, part_b), ('win', 'seq'))  99.7 us
    ppermute x3, waiting for transfers between devices, passed_along(): return lax.ppermute(value, axis, pairs)  63.8 us
    psum x1, blocking collectives, on_device(): lax.psum((input_piece, backward_piece), 'chan')  28.9 us
    dot_general x4, matrix products, transform(): jnp.einsum('ft,wtc->wfc', table, block, precision=highest, preferred_elem...  21.3 us
    unnamed x34, local copies, waits for them, and re-layouts  10.4 us
    dot_general x4, matrix products, on_device(): jnp.dot(table, block, precision=highest, preferred_element_type=jnp.float32)  5.85 us
  transfers between devices with their start and end apart: 5, of which 4 were waited for; matrix products, arithmetic and copies ran while one was open for 16% of the time, Pallas kernels for 0%

commit v1 on v0

v1 whole, which is shorter than its diff:
```python
import functools
import math

import jax
import jax.numpy as jnp
import ml_dtypes
import numpy as np
from jax import lax
from jax.experimental import pallas as pl
from jax.experimental.pallas import tpu as pltpu
from jax.sharding import PartitionSpec as P

MESH = pl.DeviceIdType.MESH
bf16 = jnp.bfloat16
f32 = jnp.float32

ROWS = 256
CH = 512
Q = 128
RANK = 64
SEQ = 4
XS = 4
ZS = 8
YS = 8
SL = 2 * RANK // ZS


def fourier_table():
    k = np.arange(ROWS)[:, None]
    t = np.arange(ROWS)[None, :]
    angle = 2.0 * math.pi / (2 * ROWS) * ((2 * k + 1) * t % (4 * ROWS)) / 2.0
    return np.concatenate([np.cos(angle), -np.sin(angle)], axis=0)


def in_two(table):
    high = table.astype(ml_dtypes.bfloat16)
    return high, (table - high.astype(np.float64)).astype(ml_dtypes.bfloat16)


def nt(a, b):
    return lax.dot_general(a, b, (((1,), (1,)), ((), ())), preferred_element_type=f32)


def nn(a, b):
    return lax.dot_general(a, b, (((1,), (0,)), ((), ())), preferred_element_type=f32)


def tn(a, b):
    return lax.dot_general(a, b, (((0,), (0,)), ((), ())), preferred_element_type=f32)


def lanes(i):
    return pl.ds(pl.multiple_of(i * Q, Q), Q)


def kernel(
    factor,
    second_h, conv_h, og_h, frozen_h, filt_h, down_h, up_h, tab_h, itab_h,
    two_h, ab_h,
    second, conv, og, frozen, filt, down, up, tab, itab,
    gm, gx2, ab, gated, pq, pq_in, xs, pqb, fs, gs_send, gs, hs, xf, ys, rs_send, rs,
    ab_send, zr, yr, fin,
    load_sem, core_ss, core_rs, x_ss, x_rs, f_ss, f_rs, g_ss, g_rs, r_ss, r_rs, z_ss, z_rs, y_ss, y_rs, n_ss, n_rs, out_sem,
):
    w = lax.axis_index("win")
    s = lax.axis_index("seq")
    c = lax.axis_index("chan")
    ylo, z = w // ZS, lax.rem(w, ZS)
    y = s * 2 + ylo
    x, core = c // 2, lax.rem(c, 2)

    def at_core():
        return (w, s, x * 2 + 1 - core)

    def at_x(d):
        return (w, s, lax.rem(x + d, XS) * 2 + core)

    def at_seq(d):
        return (w, lax.rem(s + d, SEQ), c)

    def at_z(d):
        return (ylo * ZS + lax.rem(z + d, ZS), s, c)

    def at_y(d):
        other = lax.rem(y + d, YS)
        return (lax.rem(other, 2) * ZS + z, other // 2, c)

    far_x = (2, 1, 3)
    far_seq = (2, 1, 3)
    far_z = (4, 3, 5, 2, 6, 1, 7)
    partners = [at_core()] + [at_x(d) for d in far_x] + [at_z(d) for d in far_z] + [at_y(d) for d in far_z]
    barrier = pltpu.get_barrier_semaphore()
    for p in partners:
        pl.semaphore_signal(barrier, inc=1, device_id=p, device_id_type=MESH)

    loads = {}
    pairs = (
        ("og", og_h, og), ("up", up_h, up), ("second", second_h, second), ("conv", conv_h, conv),
        ("down", down_h, down), ("filt", filt_h, filt), ("frozen", frozen_h, frozen),
        ("tab", tab_h, tab), ("itab", itab_h, itab),
    )
    for i, (name, src, dst) in enumerate(pairs):
        loads[name] = pltpu.make_async_copy(src, dst, load_sem.at[i])
        loads[name].start()

    def remote(src, dst, ss, rs_, dev):
        return pltpu.make_async_remote_copy(
            src_ref=src, dst_ref=dst, send_sem=ss, recv_sem=rs_, device_id=dev, device_id_type=MESH
        )

    def keep(part, base):
        packed = jnp.concatenate([part[: ROWS // 2], part[ROWS // 2 :]], axis=1)
        pq[0, base : base + 64] = packed[:64]
        pq[1, base : base + 64] = packed[64:]

    loads["og"].wait()
    loads["up"].wait()
    keep(nt(og[...], up[...]), 0)
    loads["second"].wait()
    loads["conv"].wait()
    loads["down"].wait()
    gated[...] = (second[...].astype(f32) * conv[...].astype(f32)).astype(bf16)
    keep(nt(gated[...], down[...]), 64)
    loads["filt"].wait()

    pl.semaphore_wait(barrier, len(partners))

    core_a = remote(pq.at[1 - core], pq_in, core_ss.at[0], core_rs.at[0], at_core())
    core_a.start()
    f_copies = []
    for d in far_seq:
        cp = remote(filt.at[:, lanes(lax.rem(s + d, SEQ))], fs.at[s], f_ss.at[d], f_rs.at[d], at_seq(d))
        cp.start()
        f_copies.append(cp)
    core_a.wait_recv()
    xs[x] = pq[core] + pq_in[...]
    x_copies = []
    for d in far_x:
        cp = remote(xs.at[x], xs.at[x], x_ss.at[d], x_rs.at[d], at_x(d))
        cp.start()
        x_copies.append(cp)
    fs[s] = filt[:, lanes(s)]
    for n in ("frozen", "tab", "itab"):
        loads[n].wait()
    for cp in x_copies:
        cp.wait_recv()
    pqb[core] = ((xs[0] + xs[1]) + (xs[2] + xs[3])).astype(bf16)
    core_b = remote(pqb.at[core], pqb.at[core], core_ss.at[1], core_rs.at[1], at_core())
    core_b.start()
    core_b.wait_recv()

    def unpack(base):
        both = jnp.concatenate([pqb[0, base : base + 64], pqb[1, base : base + 64]], axis=0)
        return jnp.concatenate([both[:, :RANK], both[:, RANK:]], axis=0)

    low_back = unpack(0)
    low_in = unpack(64)

    def grad_conv(q):
        gg = frozen[:, lanes(q)].astype(f32) + 2.0 * nn(low_back, down[:, lanes(q)])
        gx2[:, lanes(q)] = (gg * conv[:, lanes(q)].astype(f32)).astype(bf16)
        return (gg * second[:, lanes(q)].astype(f32)).astype(bf16)

    g_copies = []
    for i, d in enumerate(far_seq):
        gs_send[i] = grad_conv(lax.rem(s + d, SEQ))
        cp = remote(gs_send.at[i], gs.at[s], g_ss.at[d], g_rs.at[d], at_seq(d))
        cp.start()
        g_copies.append(cp)

    part_a = tn(low_back, gated[...]).astype(bf16)
    part_b = tn(low_in, og[...]).astype(bf16)
    for i in range(ZS // 2):
        ab_send[i] = part_a[SL * i : SL * (i + 1)]
        ab_send[ZS // 2 + i] = part_b[SL * i : SL * (i + 1)]
    z_copies = []
    for d in far_z:
        cp = remote(ab_send.at[lax.rem(z + d, ZS)], zr.at[z], z_ss.at[d], z_rs.at[d], at_z(d))
        cp.start()
        z_copies.append(cp)
    zr[z] = ab_send[z]
    gs[s] = grad_conv(s)
    out_copies = [pltpu.make_async_copy(gx2, two_h.at[pl.ds(ROWS, ROWS)], out_sem.at[0])]
    out_copies[0].start()

    def transform(block):
        both = nn(tab[...], block)
        return both[: 2 * ROWS] + both[2 * ROWS :]

    for cp in f_copies:
        cp.wait_recv()
    sign = (1 - 2 * lax.rem(lax.broadcasted_iota(jnp.int32, (ROWS, Q), 0), 2)).astype(f32)
    before = None
    for lag in range(SEQ):
        spec = transform(fs[lag])
        re, im = spec[:ROWS], spec[ROWS:]
        if before is None:
            hs[lag, :ROWS] = re
            hs[lag, ROWS:] = im
        else:
            hs[lag, :ROWS] = re - sign * before[1]
            hs[lag, ROWS:] = im + sign * before[0]
        before = (re, im)

    for cp in z_copies:
        cp.wait_recv()
    total = zr[0].astype(f32)
    for i in range(1, ZS):
        total = total + zr[i].astype(f32)
    yr[y] = total.astype(bf16)
    y_copies = []
    for d in far_z:
        cp = remote(yr.at[y], yr.at[y], y_ss.at[d], y_rs.at[d], at_y(d))
        cp.start()
        y_copies.append(cp)

    for cp in g_copies:
        cp.wait_recv()
    for i in range(SEQ):
        xf[i] = transform(gs[i])
    for j in range(SEQ - 1, -1, -1):
        for r in range(0, ROWS, 64):
            yre = jnp.zeros((64, Q), f32)
            yim = jnp.zeros((64, Q), f32)
            for i in range(j, SEQ):
                a, b = xf[i, r : r + 64], xf[i, ROWS + r : ROWS + r + 64]
                p, q = hs[i - j, r : r + 64], hs[i - j, ROWS + r : ROWS + r + 64]
                yre = yre + a * p + b * q
                yim = yim + b * p - a * q
            ys[r : r + 64] = yre.astype(bf16)
            ys[ROWS + r : ROWS + r + 64] = yim.astype(bf16)
        spec = ys[...]
        out = (nn(itab[...], jnp.concatenate([spec, spec], axis=0)) * (1.0 / ROWS)).astype(bf16)
        rs_send[j] = out

        @pl.when(s != j)
        def _():
            d = lax.rem(j - s + SEQ, SEQ)
            remote(rs_send.at[j], rs.at[s], r_ss.at[d], r_rs.at[d], (w, j, c)).start()

    gm[:, lanes(s)] = rs_send[s]

    for cp in y_copies:
        cp.wait_recv()
    total = yr[0].astype(f32)
    for i in range(1, YS):
        total = total + yr[i].astype(f32)
    fin[z] = (total * factor).astype(bf16)
    n_copies = []
    for d in far_z:
        cp = remote(fin.at[z], fin.at[z], n_ss.at[d], n_rs.at[d], at_z(d))
        cp.start()
        n_copies.append(cp)

    r_copies = []
    for d in (1, 3, 2):
        other = lax.rem(s + d, SEQ)
        cp = remote(rs_send.at[other], rs.at[s], r_ss.at[d], r_rs.at[d], at_seq(d))
        r_copies.append(cp)
    for d, cp in zip((1, 3, 2), r_copies, strict=True):
        cp.wait_recv()
        source = lax.rem(s - d + SEQ, SEQ)
        gm[:, lanes(source)] = rs[source]
    out_copies.append(pltpu.make_async_copy(gm, two_h.at[pl.ds(0, ROWS)], out_sem.at[1]))
    out_copies[1].start()
    for cp in n_copies:
        cp.wait_recv()
    for i in range(ZS):
        ab[SL * i : SL * (i + 1)] = fin[i].astype(f32)

    out_copies.append(pltpu.make_async_copy(ab, ab_h, out_sem.at[2]))
    out_copies[2].start()
    for cp in [core_a, core_b] + f_copies + x_copies + g_copies + z_copies + y_copies + r_copies + n_copies:
        cp.wait_send()
    for cp in out_copies:
        cp.wait()


def on_device(
    first_gate_1, operator_values, second_gate_2, convolved_output, output_gradient,
    frozen_gradient, filt, adapter_down_weight, adapter_up_weight,
):
    positions = lax.axis_size("win") * first_gate_1.shape[0] * first_gate_1.shape[1] * lax.axis_size("seq")
    factor = 2.0 / math.sqrt(positions)
    table = fourier_table()
    tab = jnp.asarray(np.concatenate(in_two(table), axis=0))
    itab = jnp.asarray(np.concatenate(in_two(np.ascontiguousarray(table.T)), axis=1))
    blk = functools.partial(pltpu.VMEM, (ROWS, CH))
    dma = pltpu.SemaphoreType.DMA
    two, ab = pl.pallas_call(
        functools.partial(kernel, factor),
        out_shape=(
            jax.ShapeDtypeStruct((2 * ROWS, CH), bf16),
            jax.ShapeDtypeStruct((2 * RANK, CH), f32),
        ),
        in_specs=[pl.BlockSpec(memory_space=pltpu.HBM)] * 9,
        out_specs=tuple([pl.BlockSpec(memory_space=pltpu.HBM)] * 2),
        scratch_shapes=[
            blk(bf16), blk(bf16), blk(bf16), blk(bf16), blk(bf16),
            pltpu.VMEM((RANK, CH), bf16), pltpu.VMEM((RANK, CH), bf16),
            pltpu.VMEM((4 * ROWS, ROWS), bf16), pltpu.VMEM((ROWS, 4 * ROWS), bf16),
            blk(bf16), blk(bf16), pltpu.VMEM((2 * RANK, CH), f32),
            blk(bf16),
            pltpu.VMEM((2, 128, 128), f32), pltpu.VMEM((128, 128), f32),
            pltpu.VMEM((XS, 128, 128), f32), pltpu.VMEM((2, 128, 128), bf16),
            pltpu.VMEM((SEQ, ROWS, Q), bf16),
            pltpu.VMEM((SEQ - 1, ROWS, Q), bf16), pltpu.VMEM((SEQ, ROWS, Q), bf16),
            pltpu.VMEM((SEQ, 2 * ROWS, Q), f32), pltpu.VMEM((SEQ, 2 * ROWS, Q), f32),
            pltpu.VMEM((2 * ROWS, Q), bf16),
            pltpu.VMEM((SEQ, ROWS, Q), bf16), pltpu.VMEM((SEQ, ROWS, Q), bf16),
            pltpu.VMEM((ZS, SL, CH), bf16), pltpu.VMEM((ZS, SL, CH), bf16),
            pltpu.VMEM((YS, SL, CH), bf16), pltpu.VMEM((ZS, SL, CH), bf16),
            dma((9,)), dma((2,)), dma((2,)), dma((XS,)), dma((XS,)),
            dma((SEQ,)), dma((SEQ,)), dma((SEQ,)), dma((SEQ,)), dma((SEQ,)), dma((SEQ,)),
            dma((ZS,)), dma((ZS,)), dma((YS,)), dma((YS,)), dma((ZS,)), dma((ZS,)), dma((3,)),
        ],
        compiler_params=pltpu.CompilerParams(
            collective_id=0, has_side_effects=True, vmem_limit_bytes=60 * 1024 * 1024
        ),
        name="window_backward",
    )(
        second_gate_2[0], convolved_output[0], output_gradient[0], frozen_gradient[0], filt,
        adapter_down_weight.T, adapter_up_weight, tab, itab,
    )
    gm = two[:ROWS].astype(f32)
    grad_x1 = (gm * operator_values[0].astype(f32)).astype(bf16)
    grad_values = (gm * first_gate_1[0].astype(f32)).astype(bf16)
    return grad_x1[None], grad_values[None], two[ROWS:][None], ab[:RANK].T, ab[RANK:]


def solution(mesh):
    block = P("win", "seq", "chan")
    in_specs = (block,) * 6 + (P("seq", "chan"), P("chan", None), P(None, "chan"))
    out_specs = (block,) * 3 + (P("chan", None), P(None, "chan"))
    return jax.shard_map(
        on_device, mesh=mesh, in_specs=in_specs, out_specs=out_specs, check_vma=False
    )
```

time: 267 us -> 47.3 us (0.18); the launches traced: 263 us -> 47.1 us
  waiting for transfers between devices: 164 us -> 0 us
  Pallas kernels: 0 us -> 42.7 us
  matrix products: 35.3 us -> 0 us
  blocking collectives: 28.9 us -> 0 us
  between operations: 15.7 us -> 0.66 us
  local copies, waits for them, and re-layouts: 10.4 us -> 2.87 us
  starting transfers between devices: 4.1 us -> 0 us
  other arithmetic: 4.09 us -> 0.9 us
    psum x1 -> x0, waiting for transfers between devices: 99.7 us -> none  [on_device(): grad_a, grad_b = lax.psum((part_a, part_b), ('win', 'seq'))]
    ppermute x3 -> x0, waiting for transfers between devices: 63.8 us -> none  [passed_along(): return lax.ppermute(value, axis, pairs)]
    pallas_call x0 -> x1, Pallas kernels: none -> 42.7 us  [on_device(): pl.pallas_call(functools.partial(kernel, factor), out_shape=(jax.ShapeDty...]
    dot_general x14 -> x0, matrix products: 35.3 us -> none  [the longest x4 21.3 us: transform(): jnp.einsum('ft,wtc->wfc', table, block, precision=highest, preferred_elem...]
    psum x1 -> x0, blocking collectives: 28.9 us -> none  [on_device(): lax.psum((input_piece, backward_piece), 'chan')]
    unnamed x34 -> x6, local copies, waits for them, and re-layouts: 10.4 us -> 0.4 us
    ppermute x3 -> x0, starting transfers between devices: 4.02 us -> none  [passed_along(): return lax.ppermute(value, axis, pairs)]
  transfers between devices with their start and end apart: 5 -> 0, of which waited for: 4 -> 0; matrix products, arithmetic and copies ran while one was open for 16% -> 0% of each run, Pallas kernels for 0% -> 0%
where the time goes in v1:
time: 47.3 us; the launch traced here: 47.1 us
  Pallas kernels  42.7 us (90%)
  local copies, waits for them, and re-layouts  2.87 us (6%)
  other arithmetic  0.9 us (2%)
  between operations  0.66 us (1%)
    pallas_call x1, Pallas kernels, on_device(): pl.pallas_call(functools.partial(kernel, factor), out_shape=(jax.ShapeDty...  42.7 us
    slice x1, local copies, waits for them, and re-layouts, on_device(): ab[RANK:]  1.74 us

profile of v1, /device:TPU:1, one launch (start us, length us, event | category | flops | bytes accessed | tf_op | source)
XLA Modules:
  0.0 47.1 jit_solution(8123008587488800257)
XLA Ops:
  0.6 42.7 %window_backward.1 = (bf16[512,512]{1,0:T(8,128)(2,1)}, f32[128,512]{1,0:T(8,128)}) custom-call(bf16[256,512]{1,0:T(8,128)(2,1)} %bitcast.19, bf16[256,512]{1,0:T(8,128)(2,1)} %bitcast.20, bf16[256,512]{1,0:T(8,128)(2,1)} %bitcast.21, bf16[256,512]{1,0:T(8,128)(2,1)} %bitcast.22, bf16[256,512]{1,0:T(8,128)(2,1)} %filt_h.1, bf16[64,512]{1,0:T(8,128)(2,1)} %bitcast.23, ...), custom_call_target="tpu_custom_call" | custom-call | tf_op jit(solution)/shard_map/window_backward/pallas_call | solution.py:290
  43.3 0.0 copy-start
  43.3 1.7 %fusion.4 = (f32[64,512]{1,0:T(8,128)}, f32[512,64]{0,1:T(8,128)}) fusion(f32[128,512]{1,0:T(8,128)} %get-tuple-element.8), kind=kLoop, calls=%fused_computation.8 | loop fusion | bytes 524288 | tf_op jit(solution)/shard_map/slice | solution.py:328
  45.1 0.0 copy-done
  45.1 0.0 copy-start.1
  45.1 0.0 copy-start.2
  45.1 0.7 %slice_bitcast_fusion = bf16[1,256,512]{2,1,0:T(8,128)(2,1)} fusion(bf16[512,512]{1,0:T(8,128)(2,1)S(1)} %copy-done), kind=kLoop, calls=%fused_computation.6 | loop fusion | bytes 524288 | tf_op jit(solution)/shard_map/broadcast_in_dim | solution.py:328
  45.8 0.3 copy-done.1
  46.1 0.1 copy-done.2
  46.2 0.9 %fusion.2 = (bf16[1,256,512]{2,1,0:T(8,128)(2,1)}, bf16[1,256,512]{2,1,0:T(8,128)(2,1)}) fusion(bf16[1,256,512]{2,1,0:T(8,128)(2,1)S(1)} %copy-done.1, bf16[512,512]{1,0:T(8,128)(2,1)S(1)} %copy-done, bf16[1,256,512]{2,1,0:T(8,128)(2,1)S(1)} %copy-done.2), kind=kLoop, calls=%fused_computation.4 | loop fusion | flops 917504 | bytes 1310720 | tf_op jit(solution)/shard_map/broadcast_in_dim | solution.py:328
Async XLA Ops:
  43.3 1.8 %copy-start = (bf16[512,512]{1,0:T(8,128)(2,1)S(1)}, bf16[512,512]{1,0:T(8,128)(2,1)}, u32[]{:S(2)}) copy-start(bf16[512,512]{1,0:T(8,128)(2,1)} %get-tuple-element.7) | copy-start | bytes 1572868
  45.1 1.0 %copy-start.1 = (bf16[1,256,512]{2,1,0:T(8,128)(2,1)S(1)}, bf16[1,256,512]{2,1,0:T(8,128)(2,1)}, u32[]{:S(2)}) copy-start(bf16[1,256,512]{2,1,0:T(8,128)(2,1)} %param.11) | copy-start | bytes 786436
  45.1 1.1 %copy-start.2 = (bf16[1,256,512]{2,1,0:T(8,128)(2,1)S(1)}, bf16[1,256,512]{2,1,0:T(8,128)(2,1)}, u32[]{:S(2)}) copy-start(bf16[1,256,512]{2,1,0:T(8,128)(2,1)} %param.12) | copy-start | bytes 786436

commit v2 on v1

--- a/solution.py
+++ b/solution.py
@@ -56,9 +56,9 @@
 def kernel(
     factor,
     second_h, conv_h, og_h, frozen_h, filt_h, down_h, up_h, tab_h, itab_h,
-    two_h, ab_h,
+    gm_h, gx2_h, fin_h,
     second, conv, og, frozen, filt, down, up, tab, itab,
-    gm, gx2, ab, gated, pq, pq_in, xs, pqb, fs, gs_send, gs, hs, xf, ys, rs_send, rs,
+    gx2, gated, pq, pq_in, xs, pqb, fs, gs_send, gs, hs, xf, ys, rs_send,
     ab_send, zr, yr, fin,
     load_sem, core_ss, core_rs, x_ss, x_rs, f_ss, f_rs, g_ss, g_rs, r_ss, r_rs, z_ss, z_rs, y_ss, y_rs, n_ss, n_rs, out_sem,
 ):
@@ -133,7 +133,7 @@
         cp.start()
         f_copies.append(cp)
     core_a.wait_recv()
-    xs[x] = pq[core] + pq_in[...]
+    xs[x] = (pq[core] + pq_in[...]).astype(bf16)
     x_copies = []
     for d in far_x:
         cp = remote(xs.at[x], xs.at[x], x_ss.at[d], x_rs.at[d], at_x(d))
@@ -144,7 +144,8 @@
         loads[n].wait()
     for cp in x_copies:
         cp.wait_recv()
-    pqb[core] = ((xs[0] + xs[1]) + (xs[2] + xs[3])).astype(bf16)
+    parts = [xs[i].astype(f32) for i in range(XS)]
+    pqb[core] = ((parts[0] + parts[1]) + (parts[2] + parts[3])).astype(bf16)
     core_b = remote(pqb.at[core], pqb.at[core], core_ss.at[1], core_rs.at[1], at_core())
     core_b.start()
     core_b.wait_recv()
@@ -160,13 +161,6 @@
         gg = frozen[:, lanes(q)].astype(f32) + 2.0 * nn(low_back, down[:, lanes(q)])
         gx2[:, lanes(q)] = (gg * conv[:, lanes(q)].astype(f32)).astype(bf16)
         return (gg * second[:, lanes(q)].astype(f32)).astype(bf16)
-
-    g_copies = []
-    for i, d in enumerate(far_seq):
-        gs_send[i] = grad_conv(lax.rem(s + d, SEQ))
-        cp = remote(gs_send.at[i], gs.at[s], g_ss.at[d], g_rs.at[d], at_seq(d))
-        cp.start()
-        g_copies.append(cp)
 
     part_a = tn(low_back, gated[...]).astype(bf16)
     part_b = tn(low_in, og[...]).astype(bf16)
@@ -179,28 +173,40 @@
         cp.start()
         z_copies.append(cp)
     zr[z] = ab_send[z]
+    g_copies = []
+    for i, d in enumerate(far_seq):
+        gs_send[i] = grad_conv(lax.rem(s + d, SEQ))
+        cp = remote(gs_send.at[i], gs.at[s], g_ss.at[d], g_rs.at[d], at_seq(d))
+        cp.start()
+        g_copies.append(cp)
+
     gs[s] = grad_conv(s)
-    out_copies = [pltpu.make_async_copy(gx2, two_h.at[pl.ds(ROWS, ROWS)], out_sem.at[0])]
+    out_copies = [pltpu.make_async_copy(gx2, gx2_h, out_sem.at[0])]
     out_copies[0].start()
 
-    def transform(block):
-        both = nn(tab[...], block)
-        return both[: 2 * ROWS] + both[2 * ROWS :]
+    def transform(src, dst, i, j):
+        both = jnp.concatenate([src[i], src[j]], axis=1)
+        spec = nn(tab[...], jnp.concatenate([both, both], axis=0))
+        dst[i] = spec[:, :Q]
+        dst[j] = spec[:, Q:]
 
     for cp in f_copies:
         cp.wait_recv()
-    sign = (1 - 2 * lax.rem(lax.broadcasted_iota(jnp.int32, (ROWS, Q), 0), 2)).astype(f32)
-    before = None
-    for lag in range(SEQ):
-        spec = transform(fs[lag])
-        re, im = spec[:ROWS], spec[ROWS:]
-        if before is None:
-            hs[lag, :ROWS] = re
-            hs[lag, ROWS:] = im
-        else:
-            hs[lag, :ROWS] = re - sign * before[1]
-            hs[lag, ROWS:] = im + sign * before[0]
-        before = (re, im)
+
+    @pl.loop(0, SEQ // 2)
+    def _(i):
+        transform(fs, hs, 2 * i, 2 * i + 1)
+
+    sign = (1 - 2 * lax.rem(lax.broadcasted_iota(jnp.int32, (64, Q), 0), 2)).astype(f32)
+
+    @pl.loop(0, ROWS // 64)
+    def _(r):
+        up_rows = pl.ds(pl.multiple_of(r * 64, 64), 64)
+        low_rows = pl.ds(pl.multiple_of(ROWS + r * 64, 64), 64)
+        spec = [(hs[lag, up_rows], hs[lag, low_rows]) for lag in range(SEQ)]
+        for lag in range(1, SEQ):
+            hs[lag, up_rows] = spec[lag][0] - sign * spec[lag - 1][1]
+            hs[lag, low_rows] = spec[lag][1] + sign * spec[lag - 1][0]
 
     for cp in z_copies:
         cp.wait_recv()
@@ -214,65 +220,111 @@
         cp.start()
         y_copies.append(cp)
 
-    for cp in g_copies:
-        cp.wait_recv()
-    for i in range(SEQ):
-        xf[i] = transform(gs[i])
-    for j in range(SEQ - 1, -1, -1):
-        for r in range(0, ROWS, 64):
-            yre = jnp.zeros((64, Q), f32)
-            yim = jnp.zeros((64, Q), f32)
-            for i in range(j, SEQ):
-                a, b = xf[i, r : r + 64], xf[i, ROWS + r : ROWS + r + 64]
-                p, q = hs[i - j, r : r + 64], hs[i - j, ROWS + r : ROWS + r + 64]
-                yre = yre + a * p + b * q
-                yim = yim + b * p - a * q
-            ys[r : r + 64] = yre.astype(bf16)
-            ys[ROWS + r : ROWS + r + 64] = yim.astype(bf16)
+    g_by = dict(zip(far_seq, g_copies, strict=True))
+
+    def from_seq(d):
+        return lax.rem(s - d + SEQ, SEQ)
+
+    g_by[1].wait_recv()
+    transform(gs, xf, s, from_seq(1))
+    g_by[3].wait_recv()
+    g_by[2].wait_recv()
+    transform(gs, xf, from_seq(3), from_seq(2))
+    r_copies = []
+    for pair in ((2, 1), (3, 0)):
+        blocks = [lax.rem(s + d, SEQ) for d in pair]
+
+        @pl.loop(0, ROWS // 64)
+        def _(r):
+            up_rows = pl.ds(pl.multiple_of(r * 64, 64), 64)
+            low_rows = pl.ds(pl.multiple_of(ROWS + r * 64, 64), 64)
+            for side, j in enumerate(blocks):
+
+                def add(i, sums):
+                    a, b = xf[i, up_rows], xf[i, low_rows]
+                    p, q = hs[i - j, up_rows], hs[i - j, low_rows]
+                    return sums[0] + a * p + b * q, sums[1] + b * p - a * q
+
+                zeros = jnp.zeros((64, Q), f32)
+                yre, yim = lax.fori_loop(j, SEQ, add, (zeros, zeros))
+                ys[up_rows, side * Q : side * Q + Q] = yre.astype(bf16)
+                ys[low_rows, side * Q : side * Q + Q] = yim.astype(bf16)
+
         spec = ys[...]
         out = (nn(itab[...], jnp.concatenate([spec, spec], axis=0)) * (1.0 / ROWS)).astype(bf16)
-        rs_send[j] = out
-
-        @pl.when(s != j)
-        def _():
-            d = lax.rem(j - s + SEQ, SEQ)
-            remote(rs_send.at[j], rs.at[s], r_ss.at[d], r_rs.at[d], (w, j, c)).start()
-
-    gm[:, lanes(s)] = rs_send[s]
+        for side, d in enumerate(pair):
+            rs_send[d] = out[:, side * Q : side * Q + Q]
+            if d:
+                cp = remote(rs_send.at[d], gm_h.at[s], r_ss.at[d], r_rs.at[d], at_seq(d))
+                r_copies.append(cp)
+            else:
+                cp = pltpu.make_async_copy(rs_send.at[d], gm_h.at[s], out_sem.at[1])
+                out_copies.append(cp)
+            cp.start()
 
     for cp in y_copies:
         cp.wait_recv()
     total = yr[0].astype(f32)
     for i in range(1, YS):
         total = total + yr[i].astype(f32)
-    fin[z] = (total * factor).astype(bf16)
+    fin[...] = (total * factor).astype(bf16)
     n_copies = []
     for d in far_z:
-        cp = remote(fin.at[z], fin.at[z], n_ss.at[d], n_rs.at[d], at_z(d))
+        cp = remote(fin, fin_h.at[z], n_ss.at[d], n_rs.at[d], at_z(d))
         cp.start()
         n_copies.append(cp)
 
-    r_copies = []
-    for d in (1, 3, 2):
-        other = lax.rem(s + d, SEQ)
-        cp = remote(rs_send.at[other], rs.at[s], r_ss.at[d], r_rs.at[d], at_seq(d))
-        r_copies.append(cp)
-    for d, cp in zip((1, 3, 2), r_copies, strict=True):
-        cp.wait_recv()
-        source = lax.rem(s - d + SEQ, SEQ)
-        gm[:, lanes(source)] = rs[source]
-    out_copies.append(pltpu.make_async_copy(gm, two_h.at[pl.ds(0, ROWS)], out_sem.at[1]))
-    out_copies[1].start()
-    for cp in n_copies:
-        cp.wait_recv()
-    for i in range(ZS):
-        ab[SL * i : SL * (i + 1)] = fin[i].astype(f32)
-
-    out_copies.append(pltpu.make_async_copy(ab, ab_h, out_sem.at[2]))
-    out_copies[2].start()
+    out_copies.append(pltpu.make_async_copy(fin, fin_h.at[z], out_sem.at[2]))
+    out_copies[-1].start()
+
+    for cp in r_copies + n_copies:
+        cp.wait_recv()
     for cp in [core_a, core_b] + f_copies + x_copies + g_copies + z_copies + y_copies + r_copies + n_copies:
         cp.wait_send()
     for cp in out_copies:
+        cp.wait()
+
+
+def results_kernel(
+    gm_h, gx2_h, fin_h, values_h, first_h, x1_h, val_h, x2_h, a_h, b_h,
+    gm, values, first, x1, val, x2, fin, low, in_sem, out_sem,
+):
+    halves = [pl.ds(0, ROWS // 2), pl.ds(ROWS // 2, ROWS // 2)]
+    loads = []
+    stores = []
+
+    def fetch(src, dst):
+        loads.append(pltpu.make_async_copy(src, dst, in_sem.at[len(loads)]))
+        loads[-1].start()
+
+    def put(src, dst):
+        stores.append(pltpu.make_async_copy(src, dst, out_sem.at[len(stores)]))
+        stores[-1].start()
+
+    for rows in halves:
+        fetch(gm_h.at[:, rows], gm.at[:, rows])
+        fetch(values_h.at[rows], values.at[rows])
+        fetch(first_h.at[rows], first.at[rows])
+    fetch(gx2_h, x2)
+    fetch(fin_h, fin)
+    for i, rows in enumerate(halves):
+        for cp in loads[3 * i : 3 * i + 3]:
+            cp.wait()
+        for q in range(SEQ):
+            cols = slice(q * Q, q * Q + Q)
+            mixed = gm[q, rows].astype(f32)
+            x1[rows, cols] = (mixed * values[rows, cols].astype(f32)).astype(bf16)
+            val[rows, cols] = (mixed * first[rows, cols].astype(f32)).astype(bf16)
+        put(x1.at[rows], x1_h.at[rows])
+        put(val.at[rows], val_h.at[rows])
+    for cp in loads[6:]:
+        cp.wait()
+    put(x2, x2_h)
+    for i in range(ZS):
+        low[SL * i : SL * (i + 1)] = fin[i].astype(f32)
+    put(low.at[pl.ds(0, RANK)], a_h)
+    put(low.at[pl.ds(RANK, RANK)], b_h)
+    for cp in stores:
         cp.wait()
 
 
@@ -283,33 +335,34 @@
     positions = lax.axis_size("win") * first_gate_1.shape[0] * first_gate_1.shape[1] * lax.axis_size("seq")
     factor = 2.0 / math.sqrt(positions)
     table = fourier_table()
-    tab = jnp.asarray(np.concatenate(in_two(table), axis=0))
+    tab = jnp.asarray(np.concatenate(in_two(table), axis=1))
     itab = jnp.asarray(np.concatenate(in_two(np.ascontiguousarray(table.T)), axis=1))
     blk = functools.partial(pltpu.VMEM, (ROWS, CH))
     dma = pltpu.SemaphoreType.DMA
-    two, ab = pl.pallas_call(
+    mixed, grad_x2, slices = pl.pallas_call(
         functools.partial(kernel, factor),
         out_shape=(
-            jax.ShapeDtypeStruct((2 * ROWS, CH), bf16),
-            jax.ShapeDtypeStruct((2 * RANK, CH), f32),
+            jax.ShapeDtypeStruct((SEQ, ROWS, Q), bf16),
+            jax.ShapeDtypeStruct((ROWS, CH), bf16),
+            jax.ShapeDtypeStruct((ZS, SL, CH), bf16),
         ),
         in_specs=[pl.BlockSpec(memory_space=pltpu.HBM)] * 9,
-        out_specs=tuple([pl.BlockSpec(memory_space=pltpu.HBM)] * 2),
+        out_specs=tuple([pl.BlockSpec(memory_space=pltpu.HBM)] * 3),
         scratch_shapes=[
             blk(bf16), blk(bf16), blk(bf16), blk(bf16), blk(bf16),
             pltpu.VMEM((RANK, CH), bf16), pltpu.VMEM((RANK, CH), bf16),
-            pltpu.VMEM((4 * ROWS, ROWS), bf16), pltpu.VMEM((ROWS, 4 * ROWS), bf16),
-            blk(bf16), blk(bf16), pltpu.VMEM((2 * RANK, CH), f32),
+            pltpu.VMEM((2 * ROWS, 2 * ROWS), bf16), pltpu.VMEM((ROWS, 4 * ROWS), bf16),
+            blk(bf16),
             blk(bf16),
             pltpu.VMEM((2, 128, 128), f32), pltpu.VMEM((128, 128), f32),
-            pltpu.VMEM((XS, 128, 128), f32), pltpu.VMEM((2, 128, 128), bf16),
+            pltpu.VMEM((XS, 128, 128), bf16), pltpu.VMEM((2, 128, 128), bf16),
             pltpu.VMEM((SEQ, ROWS, Q), bf16),
             pltpu.VMEM((SEQ - 1, ROWS, Q), bf16), pltpu.VMEM((SEQ, ROWS, Q), bf16),
             pltpu.VMEM((SEQ, 2 * ROWS, Q), f32), pltpu.VMEM((SEQ, 2 * ROWS, Q), f32),
-            pltpu.VMEM((2 * ROWS, Q), bf16),
-            pltpu.VMEM((SEQ, ROWS, Q), bf16), pltpu.VMEM((SEQ, ROWS, Q), bf16),
+            pltpu.VMEM((2 * ROWS, 2 * Q), bf16),
+            pltpu.VMEM((SEQ, ROWS, Q), bf16),
             pltpu.VMEM((ZS, SL, CH), bf16), pltpu.VMEM((ZS, SL, CH), bf16),
-            pltpu.VMEM((YS, SL, CH), bf16), pltpu.VMEM((ZS, SL, CH), bf16),
+            pltpu.VMEM((YS, SL, CH), bf16), pltpu.VMEM((SL, CH), bf16),
             dma((9,)), dma((2,)), dma((2,)), dma((XS,)), dma((XS,)),
             dma((SEQ,)), dma((SEQ,)), dma((SEQ,)), dma((SEQ,)), dma((SEQ,)), dma((SEQ,)),
             dma((ZS,)), dma((ZS,)), dma((YS,)), dma((YS,)), dma((ZS,)), dma((ZS,)), dma((3,)),
@@ -322,10 +375,19 @@
         second_gate_2[0], convolved_output[0], output_gradient[0], frozen_gradient[0], filt,
         adapter_down_weight.T, adapter_up_weight, tab, itab,
     )
-    gm = two[:ROWS].astype(f32)
-    grad_x1 = (gm * operator_values[0].astype(f32)).astype(bf16)
-    grad_values = (gm * first_gate_1[0].astype(f32)).astype(bf16)
-    return grad_x1[None], grad_values[None], two[ROWS:][None], ab[:RANK].T, ab[RANK:]
+    wide = jax.ShapeDtypeStruct((ROWS, CH), bf16)
+    low = jax.ShapeDtypeStruct((RANK, CH), f32)
+    grad_x1, grad_values, grad_x2, grad_a, grad_b = pl.pallas_call(
+        results_kernel,
+        out_shape=(wide, wide, wide, low, low),
+        in_specs=[pl.BlockSpec(memory_space=pl.ANY)] * 5,
+        out_specs=tuple([pl.BlockSpec(memory_space=pl.ANY)] * 5),
+        scratch_shapes=[pltpu.VMEM((SEQ, ROWS, Q), bf16)] + [blk(bf16)] * 5
+        + [pltpu.VMEM((ZS, SL, CH), bf16), pltpu.VMEM((2 * RANK, CH), f32), dma((8,)), dma((7,))],
+        compiler_params=pltpu.CompilerParams(vmem_limit_bytes=60 * 1024 * 1024),
+        name="results",
+    )(mixed, grad_x2, slices, operator_values[0], first_gate_1[0])
+    return grad_x1[None], grad_values[None], grad_x2[None], grad_a.T, grad_b
 
 
 def solution(mesh):

time: 47.3 us -> 42.9 us (0.907)
  local copies, waits for them, and re-layouts: 2.87 us -> 0 us
  other arithmetic: 0.9 us -> 0 us
  Pallas kernels: 42.7 us -> 42.1 us
    pallas_call x1, Pallas kernels: 42.7 us -> 39.9 us  [on_device(): pl.pallas_call(functools.partial(kernel, factor), out_shape=(jax.ShapeDty...]
    pallas_call x0 -> x1, Pallas kernels: none -> 2.24 us  [on_device(): pl.pallas_call(results_kernel, out_shape=(wide, wide, wide, low, low), in...]
    slice x1 -> x0, local copies, waits for them, and re-layouts: 1.74 us -> none  [on_device(): ab[RANK:]]
    broadcast_in_dim x1 -> x0, other arithmetic: 0.9 us -> none  [on_device(): grad_values[None]]
    broadcast_in_dim x1 -> x0, local copies, waits for them, and re-layouts: 0.72 us -> none  [on_device(): two[ROWS:][None]]
where the time goes in v2:
time: 42.9 us; the launch traced here: 42.7 us
  Pallas kernels  42.1 us (98%)
  between operations  0.64 us (1%)
    pallas_call x1, Pallas kernels, on_device(): pl.pallas_call(functools.partial(kernel, factor), out_shape=(jax.ShapeDty...  39.9 us
    pallas_call x1, Pallas kernels, on_device(): pl.pallas_call(results_kernel, out_shape=(wide, wide, wide, low, low), in...  2.24 us

profile of v2, /device:TPU:1, one launch (start us, length us, event | category | flops | bytes accessed | tf_op | source)
XLA Modules:
  0.0 42.7 jit_solution(18094596887100568834)
XLA Ops:
  0.6 39.9 %window_backward.1 = (bf16[4,256,128]{2,1,0:T(8,128)(2,1)}, bf16[256,512]{1,0:T(8,128)(2,1)}, bf16[8,16,512]{2,1,0:T(8,128)(2,1)}) custom-call(bf16[256,512]{1,0:T(8,128)(2,1)} %bitcast.11, bf16[256,512]{1,0:T(8,128)(2,1)} %bitcast.12, bf16[256,512]{1,0:T(8,128)(2,1)} %bitcast.13, bf16[256,512]{1,0:T(8,128)(2,1)} %bitcast.14, bf16[256,512]{1,0:T(8,128)(2,1)} %filt_h.1, ...), custom_call_target="tpu_custom_call" | custom-call | tf_op jit(solution)/shard_map/window_backward/pallas_call | solution.py:342
  40.5 2.2 %results.1 = (bf16[256,512]{1,0:T(8,128)(2,1)}, bf16[256,512]{1,0:T(8,128)(2,1)}, bf16[256,512]{1,0:T(8,128)(2,1)}, f32[64,512]{1,0:T(8,128)}, f32[64,512]{1,0:T(8,128)}) custom-call(bf16[4,256,128]{2,1,0:T(8,128)(2,1)} %get-tuple-element.13.gm_h, bf16[256,512]{1,0:T(8,128)(2,1)} %get-tuple-element.14.gx2_h, bf16[8,16,512]{2,1,0:T(8,128)(2,1)} %get-tuple-element.15.fin_h, ...), custom_call_target="tpu_custom_call" | custom-call | tf_op jit(solution)/shard_map/results/pallas_call | solution.py:380

commit v3 on v2

--- a/solution.py
+++ b/solution.py
@@ -60,7 +60,7 @@
     second, conv, og, frozen, filt, down, up, tab, itab,
     gx2, gated, pq, pq_in, xs, pqb, fs, gs_send, gs, hs, xf, ys, rs_send,
     ab_send, zr, yr, fin,
-    load_sem, core_ss, core_rs, x_ss, x_rs, f_ss, f_rs, g_ss, g_rs, r_ss, r_rs, z_ss, z_rs, y_ss, y_rs, n_ss, n_rs, out_sem,
+    load_sem, core_ss, core_rs, x_ss, x_rs, f_ss, f_rs, g_ss, g_rs, r_ss, r_rs, z_ss, z_rs, y_ss, y_rs, n_ss, n_rs, out_sem, answer_sem,
 ):
     w = lax.axis_index("win")
     s = lax.axis_index("seq")
@@ -88,8 +88,16 @@
     far_x = (2, 1, 3)
     far_seq = (2, 1, 3)
     far_z = (4, 3, 5, 2, 6, 1, 7)
-    partners = [at_core()] + [at_x(d) for d in far_x] + [at_z(d) for d in far_z] + [at_y(d) for d in far_z]
+    partners = [at_core()] + [at_x(d) for d in far_x] + [at_y(d) for d in far_z]
     barrier = pltpu.get_barrier_semaphore()
+
+    def greet(semaphore, wanted):
+        for d in far_z:
+            @pl.when(wanted(lax.rem(z + d, ZS)))
+            def _():
+                pl.semaphore_signal(semaphore, inc=1, device_id=at_z(d), device_id_type=MESH)
+
+    greet(barrier, lambda other: other > z)
     for p in partners:
         pl.semaphore_signal(barrier, inc=1, device_id=p, device_id_type=MESH)
 
@@ -123,7 +131,8 @@
     keep(nt(gated[...], down[...]), 64)
     loads["filt"].wait()
 
-    pl.semaphore_wait(barrier, len(partners))
+    pl.semaphore_wait(barrier, len(partners) + z)
+    greet(answer_sem, lambda other: other < z)
 
     core_a = remote(pq.at[1 - core], pq_in, core_ss.at[0], core_rs.at[0], at_core())
     core_a.start()
@@ -167,6 +176,11 @@
     for i in range(ZS // 2):
         ab_send[i] = part_a[SL * i : SL * (i + 1)]
         ab_send[ZS // 2 + i] = part_b[SL * i : SL * (i + 1)]
+
+    @pl.when(z < ZS - 1)
+    def _():
+        pl.semaphore_wait(answer_sem, ZS - 1 - z)
+
     z_copies = []
     for d in far_z:
         cp = remote(ab_send.at[lax.rem(z + d, ZS)], zr.at[z], z_ss.at[d], z_rs.at[d], at_z(d))
@@ -366,6 +380,7 @@
             dma((9,)), dma((2,)), dma((2,)), dma((XS,)), dma((XS,)),
             dma((SEQ,)), dma((SEQ,)), dma((SEQ,)), dma((SEQ,)), dma((SEQ,)), dma((SEQ,)),
             dma((ZS,)), dma((ZS,)), dma((YS,)), dma((YS,)), dma((ZS,)), dma((ZS,)), dma((3,)),
+            pltpu.SemaphoreType.REGULAR,
         ],
         compiler_params=pltpu.CompilerParams(
             collective_id=0, has_side_effects=True, vmem_limit_bytes=60 * 1024 * 1024

time: 42.9 us -> 42 us (0.979)
  Pallas kernels: 42.1 us -> 41.2 us
    pallas_call x1, Pallas kernels: 39.9 us -> 39 us  [on_device(): pl.pallas_call(functools.partial(kernel, factor), out_shape=(jax.ShapeDty...]
where the time goes in v3:
time: 42 us; the launch traced here: 41.9 us
  Pallas kernels  41.2 us (98%)
  between operations  0.64 us (2%)
    pallas_call x1, Pallas kernels, on_device(): pl.pallas_call(functools.partial(kernel, factor), out_shape=(jax.ShapeDty...  39 us
    pallas_call x1, Pallas kernels, on_device(): pl.pallas_call(results_kernel, out_shape=(wide, wide, wide, low, low), in...  2.24 us

profile of v3, /device:TPU:1, one launch (start us, length us, event | category | flops | bytes accessed | tf_op | source)
XLA Modules:
  0.0 41.9 jit_solution(11123039897535255782)
XLA Ops:
  0.6 39.0 %window_backward.1 = (bf16[4,256,128]{2,1,0:T(8,128)(2,1)}, bf16[256,512]{1,0:T(8,128)(2,1)}, bf16[8,16,512]{2,1,0:T(8,128)(2,1)}) custom-call(bf16[256,512]{1,0:T(8,128)(2,1)} %bitcast.11, bf16[256,512]{1,0:T(8,128)(2,1)} %bitcast.12, bf16[256,512]{1,0:T(8,128)(2,1)} %bitcast.13, bf16[256,512]{1,0:T(8,128)(2,1)} %bitcast.14, bf16[256,512]{1,0:T(8,128)(2,1)} %filt_h.1, ...), custom_call_target="tpu_custom_call" | custom-call | tf_op jit(solution)/shard_map/window_backward/pallas_call | solution.py:356
  39.6 2.2 %results.1 = (bf16[256,512]{1,0:T(8,128)(2,1)}, bf16[256,512]{1,0:T(8,128)(2,1)}, bf16[256,512]{1,0:T(8,128)(2,1)}, f32[64,512]{1,0:T(8,128)}, f32[64,512]{1,0:T(8,128)}) custom-call(bf16[4,256,128]{2,1,0:T(8,128)(2,1)} %get-tuple-element.13.gm_h, bf16[256,512]{1,0:T(8,128)(2,1)} %get-tuple-element.14.gx2_h, bf16[8,16,512]{2,1,0:T(8,128)(2,1)} %get-tuple-element.15.fin_h, ...), custom_call_target="tpu_custom_call" | custom-call | tf_op jit(solution)/shard_map/results/pallas_call | solution.py:395

commit v4 on v3

--- a/solution.py
+++ b/solution.py
@@ -117,18 +117,17 @@
         )
 
     def keep(part, base):
-        packed = jnp.concatenate([part[: ROWS // 2], part[ROWS // 2 :]], axis=1)
-        pq[0, base : base + 64] = packed[:64]
-        pq[1, base : base + 64] = packed[64:]
+        for half in range(2):
+            pq[half, base : base + RANK] = part[:, half * 128 : half * 128 + 128]
 
     loads["og"].wait()
     loads["up"].wait()
-    keep(nt(og[...], up[...]), 0)
+    keep(nt(up[...], og[...]), 0)
     loads["second"].wait()
     loads["conv"].wait()
     loads["down"].wait()
     gated[...] = (second[...].astype(f32) * conv[...].astype(f32)).astype(bf16)
-    keep(nt(gated[...], down[...]), 64)
+    keep(nt(down[...], gated[...]), RANK)
     loads["filt"].wait()
 
     pl.semaphore_wait(barrier, len(partners) + z)
@@ -159,20 +158,17 @@
     core_b.start()
     core_b.wait_recv()
 
-    def unpack(base):
-        both = jnp.concatenate([pqb[0, base : base + 64], pqb[1, base : base + 64]], axis=0)
-        return jnp.concatenate([both[:, :RANK], both[:, RANK:]], axis=0)
-
-    low_back = unpack(0)
-    low_in = unpack(64)
+    low_back, low_in = (
+        jnp.concatenate([pqb[0, base : base + RANK], pqb[1, base : base + RANK]], axis=1) for base in (0, RANK)
+    )
 
     def grad_conv(q):
-        gg = frozen[:, lanes(q)].astype(f32) + 2.0 * nn(low_back, down[:, lanes(q)])
+        gg = frozen[:, lanes(q)].astype(f32) + 2.0 * tn(low_back, down[:, lanes(q)])
         gx2[:, lanes(q)] = (gg * conv[:, lanes(q)].astype(f32)).astype(bf16)
         return (gg * second[:, lanes(q)].astype(f32)).astype(bf16)
 
-    part_a = tn(low_back, gated[...]).astype(bf16)
-    part_b = tn(low_in, og[...]).astype(bf16)
+    part_a = nn(low_back, gated[...]).astype(bf16)
+    part_b = nn(low_in, og[...]).astype(bf16)
     for i in range(ZS // 2):
         ab_send[i] = part_a[SL * i : SL * (i + 1)]
         ab_send[ZS // 2 + i] = part_b[SL * i : SL * (i + 1)]
@@ -187,22 +183,69 @@
         cp.start()
         z_copies.append(cp)
     zr[z] = ab_send[z]
-    g_copies = []
-    for i, d in enumerate(far_seq):
-        gs_send[i] = grad_conv(lax.rem(s + d, SEQ))
-        cp = remote(gs_send.at[i], gs.at[s], g_ss.at[d], g_rs.at[d], at_seq(d))
-        cp.start()
-        g_copies.append(cp)
-
-    gs[s] = grad_conv(s)
-    out_copies = [pltpu.make_async_copy(gx2, gx2_h, out_sem.at[0])]
-    out_copies[0].start()
+    g_copies = [
+        remote(gs_send.at[i], gs.at[s], g_ss.at[d], g_rs.at[d], at_seq(d)) for i, d in enumerate(far_seq)
+    ]
+    r_copies = [
+        remote(rs_send.at[d], gm_h.at[s], r_ss.at[d], r_rs.at[d], at_seq(d)) for d in far_seq
+    ]
+    out_copies = [
+        pltpu.make_async_copy(gx2, gx2_h, out_sem.at[0]),
+        pltpu.make_async_copy(rs_send.at[0], gm_h.at[s], out_sem.at[1]),
+        pltpu.make_async_copy(fin, fin_h.at[z], out_sem.at[2]),
+    ]
+
+    def send_grad_conv():
+        for i, (d, cp) in enumerate(zip(far_seq, g_copies, strict=True)):
+            gs_send[i] = grad_conv(lax.rem(s + d, SEQ))
+            cp.start()
+        gs[s] = grad_conv(s)
+        out_copies[0].start()
 
     def transform(src, dst, i, j):
         both = jnp.concatenate([src[i], src[j]], axis=1)
         spec = nn(tab[...], jnp.concatenate([both, both], axis=0))
         dst[i] = spec[:, :Q]
         dst[j] = spec[:, Q:]
+
+    g_by = dict(zip(far_seq, g_copies, strict=True))
+    r_by = dict(zip(far_seq, r_copies, strict=True))
+
+    def from_seq(d):
+        return lax.rem(s - d + SEQ, SEQ)
+
+    def convolve():
+        g_by[1].wait_recv()
+        transform(gs, xf, s, from_seq(1))
+        g_by[3].wait_recv()
+        g_by[2].wait_recv()
+        transform(gs, xf, from_seq(3), from_seq(2))
+        for pair in ((2, 1), (3, 0)):
+            blocks = [lax.rem(s + d, SEQ) for d in pair]
+
+            @pl.loop(0, ROWS // 64)
+            def _(r):
+                up_rows = pl.ds(pl.multiple_of(r * 64, 64), 64)
+                low_rows = pl.ds(pl.multiple_of(ROWS + r * 64, 64), 64)
+                for side, j in enumerate(blocks):
+
+                    def add(i, sums):
+                        a, b = xf[i, up_rows], xf[i, low_rows]
+                        p, q = hs[i - j, up_rows], hs[i - j, low_rows]
+                        return sums[0] + a * p + b * q, sums[1] + b * p - a * q
+
+                    zeros = jnp.zeros((64, Q), f32)
+                    yre, yim = lax.fori_loop(j, SEQ, add, (zeros, zeros))
+                    ys[up_rows, side * Q : side * Q + Q] = yre.astype(bf16)
+                    ys[low_rows, side * Q : side * Q + Q] = yim.astype(bf16)
+
+            spec = ys[...]
+            out = (nn(itab[...], jnp.concatenate([spec, spec], axis=0)) * (1.0 / ROWS)).astype(bf16)
+            for side, d in enumerate(pair):
+                rs_send[d] = out[:, side * Q : side * Q + Q]
+                (r_by[d] if d else out_copies[1]).start()
+
+    pl.when(z < 8)(send_grad_conv)
 
     for cp in f_copies:
         cp.wait_recv()
@@ -234,48 +277,7 @@
         cp.start()
         y_copies.append(cp)
 
-    g_by = dict(zip(far_seq, g_copies, strict=True))
-
-    def from_seq(d):
-        return lax.rem(s - d + SEQ, SEQ)
-
-    g_by[1].wait_recv()
-    transform(gs, xf, s, from_seq(1))
-    g_by[3].wait_recv()
-    g_by[2].wait_recv()
-    transform(gs, xf, from_seq(3), from_seq(2))
-    r_copies = []
-    for pair in ((2, 1), (3, 0)):
-        blocks = [lax.rem(s + d, SEQ) for d in pair]
-
-        @pl.loop(0, ROWS // 64)
-        def _(r):
-            up_rows = pl.ds(pl.multiple_of(r * 64, 64), 64)
-            low_rows = pl.ds(pl.multiple_of(ROWS + r * 64, 64), 64)
-            for side, j in enumerate(blocks):
-
-                def add(i, sums):
-                    a, b = xf[i, up_rows], xf[i, low_rows]
-                    p, q = hs[i - j, up_rows], hs[i - j, low_rows]
-                    return sums[0] + a * p + b * q, sums[1] + b * p - a * q
-
-                zeros = jnp.zeros((64, Q), f32)
-                yre, yim = lax.fori_loop(j, SEQ, add, (zeros, zeros))
-                ys[up_rows, side * Q : side * Q + Q] = yre.astype(bf16)
-                ys[low_rows, side * Q : side * Q + Q] = yim.astype(bf16)
-
-        spec = ys[...]
-        out = (nn(itab[...], jnp.concatenate([spec, spec], axis=0)) * (1.0 / ROWS)).astype(bf16)
-        for side, d in enumerate(pair):
-            rs_send[d] = out[:, side * Q : side * Q + Q]
-            if d:
-                cp = remote(rs_send.at[d], gm_h.at[s], r_ss.at[d], r_rs.at[d], at_seq(d))
-                r_copies.append(cp)
-            else:
-                cp = pltpu.make_async_copy(rs_send.at[d], gm_h.at[s], out_sem.at[1])
-                out_copies.append(cp)
-            cp.start()
-
+    pl.when((z >= 0) & (z < 4))(convolve)
     for cp in y_copies:
         cp.wait_recv()
     total = yr[0].astype(f32)
@@ -288,8 +290,9 @@
         cp.start()
         n_copies.append(cp)
 
-    out_copies.append(pltpu.make_async_copy(fin, fin_h.at[z], out_sem.at[2]))
-    out_copies[-1].start()
+    out_copies[2].start()
+
+    pl.when(z >= 4)(convolve)
 
     for cp in r_copies + n_copies:
         cp.wait_recv()
@@ -303,7 +306,8 @@
     gm_h, gx2_h, fin_h, values_h, first_h, x1_h, val_h, x2_h, a_h, b_h,
     gm, values, first, x1, val, x2, fin, low, in_sem, out_sem,
 ):
-    halves = [pl.ds(0, ROWS // 2), pl.ds(ROWS // 2, ROWS // 2)]
+    parts = 2
+    halves = [pl.ds(ROWS // parts * i, ROWS // parts) for i in range(parts)]
     loads = []
     stores = []
 
@@ -315,14 +319,21 @@
         stores.append(pltpu.make_async_copy(src, dst, out_sem.at[len(stores)]))
         stores[-1].start()
 
+    fetch(gx2_h, x2)
+    fetch(fin_h, fin)
     for rows in halves:
         fetch(gm_h.at[:, rows], gm.at[:, rows])
         fetch(values_h.at[rows], values.at[rows])
         fetch(first_h.at[rows], first.at[rows])
-    fetch(gx2_h, x2)
-    fetch(fin_h, fin)
+    for cp in loads[:2]:
+        cp.wait()
+    put(x2, x2_h)
+    for i in range(ZS):
+        low[SL * i : SL * (i + 1)] = fin[i].astype(f32)
+    put(low.at[pl.ds(0, RANK)], a_h)
+    put(low.at[pl.ds(RANK, RANK)], b_h)
     for i, rows in enumerate(halves):
-        for cp in loads[3 * i : 3 * i + 3]:
+        for cp in loads[3 * i + 2 : 3 * i + 5]:
             cp.wait()
         for q in range(SEQ):
             cols = slice(q * Q, q * Q + Q)
@@ -331,13 +342,6 @@
             val[rows, cols] = (mixed * first[rows, cols].astype(f32)).astype(bf16)
         put(x1.at[rows], x1_h.at[rows])
         put(val.at[rows], val_h.at[rows])
-    for cp in loads[6:]:
-        cp.wait()
-    put(x2, x2_h)
-    for i in range(ZS):
-        low[SL * i : SL * (i + 1)] = fin[i].astype(f32)
-    put(low.at[pl.ds(0, RANK)], a_h)
-    put(low.at[pl.ds(RANK, RANK)], b_h)
     for cp in stores:
         cp.wait()
 

time: 42 us -> 41 us (0.976)
  Pallas kernels: 41.2 us -> 40.2 us
    pallas_call x1, Pallas kernels: 39 us -> 38.1 us  [on_device(): pl.pallas_call(functools.partial(kernel, factor), out_shape=(jax.ShapeDty...]
where the time goes in v4:
time: 41 us; the launch traced here: 40.9 us
  Pallas kernels  40.2 us (98%)
  between operations  0.64 us (2%)
    pallas_call x1, Pallas kernels, on_device(): pl.pallas_call(functools.partial(kernel, factor), out_shape=(jax.ShapeDty...  38.1 us
    pallas_call x1, Pallas kernels, on_device(): pl.pallas_call(results_kernel, out_shape=(wide, wide, wide, low, low), in...  2.13 us

profile of v4, /device:TPU:1, one launch (start us, length us, event | category | flops | bytes accessed | tf_op | source)
XLA Modules:
  0.0 40.9 jit_solution(18158131568757051079)
XLA Ops:
  0.6 38.1 %window_backward.1 = (bf16[4,256,128]{2,1,0:T(8,128)(2,1)}, bf16[256,512]{1,0:T(8,128)(2,1)}, bf16[8,16,512]{2,1,0:T(8,128)(2,1)}) custom-call(bf16[256,512]{1,0:T(8,128)(2,1)} %bitcast.11, bf16[256,512]{1,0:T(8,128)(2,1)} %bitcast.12, bf16[256,512]{1,0:T(8,128)(2,1)} %bitcast.13, bf16[256,512]{1,0:T(8,128)(2,1)} %bitcast.14, bf16[256,512]{1,0:T(8,128)(2,1)} %filt_h.1, ...), custom_call_target="tpu_custom_call" | custom-call | tf_op jit(solution)/shard_map/window_backward/pallas_call | solution.py:360
  38.7 2.1 %results.1 = (bf16[256,512]{1,0:T(8,128)(2,1)}, bf16[256,512]{1,0:T(8,128)(2,1)}, bf16[256,512]{1,0:T(8,128)(2,1)}, f32[64,512]{1,0:T(8,128)}, f32[64,512]{1,0:T(8,128)}) custom-call(bf16[4,256,128]{2,1,0:T(8,128)(2,1)} %get-tuple-element.13.gm_h, bf16[256,512]{1,0:T(8,128)(2,1)} %get-tuple-element.14.gx2_h, bf16[8,16,512]{2,1,0:T(8,128)(2,1)} %get-tuple-element.15.fin_h, ...), custom_call_target="tpu_custom_call" | custom-call | tf_op jit(solution)/shard_map/results/pallas_call | solution.py:399

commit v5 on v4

--- a/solution.py
+++ b/solution.py
@@ -88,19 +88,6 @@
     far_x = (2, 1, 3)
     far_seq = (2, 1, 3)
     far_z = (4, 3, 5, 2, 6, 1, 7)
-    partners = [at_core()] + [at_x(d) for d in far_x] + [at_y(d) for d in far_z]
-    barrier = pltpu.get_barrier_semaphore()
-
-    def greet(semaphore, wanted):
-        for d in far_z:
-            @pl.when(wanted(lax.rem(z + d, ZS)))
-            def _():
-                pl.semaphore_signal(semaphore, inc=1, device_id=at_z(d), device_id_type=MESH)
-
-    greet(barrier, lambda other: other > z)
-    for p in partners:
-        pl.semaphore_signal(barrier, inc=1, device_id=p, device_id_type=MESH)
-
     loads = {}
     pairs = (
         ("og", og_h, og), ("up", up_h, up), ("second", second_h, second), ("conv", conv_h, conv),
@@ -110,6 +97,19 @@
     for i, (name, src, dst) in enumerate(pairs):
         loads[name] = pltpu.make_async_copy(src, dst, load_sem.at[i])
         loads[name].start()
+
+    partners = [at_core()] + [at_x(d) for d in far_x] + [at_y(d) for d in far_z]
+    barrier = pltpu.get_barrier_semaphore()
+
+    def greet(semaphore, wanted):
+        for d in far_z:
+            @pl.when(wanted(lax.rem(z + d, ZS)))
+            def _():
+                pl.semaphore_signal(semaphore, inc=1, device_id=at_z(d), device_id_type=MESH)
+
+    greet(barrier, lambda other: other > z)
+    for p in partners:
+        pl.semaphore_signal(barrier, inc=1, device_id=p, device_id_type=MESH)
 
     def remote(src, dst, ss, rs_, dev):
         return pltpu.make_async_remote_copy(
@@ -195,12 +195,14 @@
         pltpu.make_async_copy(fin, fin_h.at[z], out_sem.at[2]),
     ]
 
-    def send_grad_conv():
-        for i, (d, cp) in enumerate(zip(far_seq, g_copies, strict=True)):
-            gs_send[i] = grad_conv(lax.rem(s + d, SEQ))
-            cp.start()
-        gs[s] = grad_conv(s)
-        out_copies[0].start()
+    @pl.loop(0, SEQ - 1)
+    def _(i):
+        d = jnp.where(i == SEQ - 2, SEQ - 1, 2 - i)
+        gs_send[i] = grad_conv(lax.rem(s + d, SEQ))
+        remote(gs_send.at[i], gs.at[s], g_ss.at[d], g_rs.at[d], at_seq(d)).start()
+
+    gs[s] = grad_conv(s)
+    out_copies[0].start()
 
     def transform(src, dst, i, j):
         both = jnp.concatenate([src[i], src[j]], axis=1)
@@ -215,12 +217,22 @@
         return lax.rem(s - d + SEQ, SEQ)
 
     def convolve():
-        g_by[1].wait_recv()
-        transform(gs, xf, s, from_seq(1))
-        g_by[3].wait_recv()
-        g_by[2].wait_recv()
-        transform(gs, xf, from_seq(3), from_seq(2))
-        for pair in ((2, 1), (3, 0)):
+        @pl.loop(0, 2)
+        def _(i):
+            @pl.when(i == 0)
+            def _():
+                g_by[1].wait_recv()
+
+            @pl.when(i == 1)
+            def _():
+                g_by[3].wait_recv()
+                g_by[2].wait_recv()
+
+            transform(gs, xf, from_seq(3 * i), from_seq(1 + i))
+
+        @pl.loop(0, 2)
+        def _(step):
+            pair = (2 + step, 1 - step)
             blocks = [lax.rem(s + d, SEQ) for d in pair]
 
             @pl.loop(0, ROWS // 64)
@@ -243,9 +255,17 @@
             out = (nn(itab[...], jnp.concatenate([spec, spec], axis=0)) * (1.0 / ROWS)).astype(bf16)
             for side, d in enumerate(pair):
                 rs_send[d] = out[:, side * Q : side * Q + Q]
-                (r_by[d] if d else out_copies[1]).start()
-
-    pl.when(z < 8)(send_grad_conv)
+            far, other = pair
+            remote(rs_send.at[far], gm_h.at[s], r_ss.at[far], r_rs.at[far], at_seq(far)).start()
+
+            @pl.when(step == 0)
+            def _():
+                r_by[1].start()
+
+            @pl.when(step == 1)
+            def _():
+                out_copies[1].start()
+
 
     for cp in f_copies:
         cp.wait_recv()
@@ -265,41 +285,45 @@
             hs[lag, up_rows] = spec[lag][0] - sign * spec[lag - 1][1]
             hs[lag, low_rows] = spec[lag][1] + sign * spec[lag - 1][0]
 
-    for cp in z_copies:
-        cp.wait_recv()
-    total = zr[0].astype(f32)
-    for i in range(1, ZS):
-        total = total + zr[i].astype(f32)
-    yr[y] = total.astype(bf16)
-    y_copies = []
-    for d in far_z:
-        cp = remote(yr.at[y], yr.at[y], y_ss.at[d], y_rs.at[d], at_y(d))
-        cp.start()
-        y_copies.append(cp)
-
-    pl.when((z >= 0) & (z < 4))(convolve)
-    for cp in y_copies:
-        cp.wait_recv()
-    total = yr[0].astype(f32)
-    for i in range(1, YS):
-        total = total + yr[i].astype(f32)
-    fin[...] = (total * factor).astype(bf16)
-    n_copies = []
-    for d in far_z:
-        cp = remote(fin, fin_h.at[z], n_ss.at[d], n_rs.at[d], at_z(d))
-        cp.start()
-        n_copies.append(cp)
-
-    out_copies[2].start()
-
-    pl.when(z >= 4)(convolve)
-
-    for cp in r_copies + n_copies:
-        cp.wait_recv()
+    y_copies = [remote(yr.at[y], yr.at[y], y_ss.at[d], y_rs.at[d], at_y(d)) for d in far_z]
+    n_copies = [remote(fin, fin_h.at[z], n_ss.at[d], n_rs.at[d], at_z(d)) for d in far_z]
+
+    def sum_z():
+        for cp in z_copies:
+            cp.wait_recv()
+        total = zr[0].astype(f32)
+        for i in range(1, ZS):
+            total = total + zr[i].astype(f32)
+        yr[y] = total.astype(bf16)
+        for cp in y_copies:
+            cp.start()
+
+    def sum_y():
+        for cp in y_copies:
+            cp.wait_recv()
+        total = yr[0].astype(f32)
+        for i in range(1, YS):
+            total = total + yr[i].astype(f32)
+        fin[...] = (total * factor).astype(bf16)
+        for cp in n_copies:
+            cp.start()
+
+        out_copies[2].start()
+
+    convolution = jnp.where(z < 4, 1, 2)
+
+    @pl.loop(0, 3)
+    def _(step):
+        pl.when(step == convolution)(convolve)
+        pl.when(step == jnp.where(convolution == 0, 1, 0))(sum_z)
+        pl.when(step == jnp.where(convolution == 2, 1, 2))(sum_y)
+
     for cp in [core_a, core_b] + f_copies + x_copies + g_copies + z_copies + y_copies + r_copies + n_copies:
         cp.wait_send()
     for cp in out_copies:
         cp.wait()
+    for cp in r_copies + n_copies:
+        cp.wait_recv()
 
 
 def results_kernel(

time: 41 us -> 41 us (level)
  no operation moved by 1% of the time
where the time goes in v5:
time: 41 us; the launch traced here: 40.9 us
  Pallas kernels  40.2 us (98%)
  between operations  0.64 us (2%)
    pallas_call x1, Pallas kernels, on_device(): pl.pallas_call(functools.partial(kernel, factor), out_shape=(jax.ShapeDty...  38.1 us
    pallas_call x1, Pallas kernels, on_device(): pl.pallas_call(results_kernel, out_shape=(wide, wide, wide, low, low), in...  2.13 us

profile of v5, /device:TPU:1, one launch (start us, length us, event | category | flops | bytes accessed | tf_op | source)
XLA Modules:
  0.0 40.9 jit_solution(18264556233330350616)
XLA Ops:
  0.6 38.1 %window_backward.1 = (bf16[4,256,128]{2,1,0:T(8,128)(2,1)}, bf16[256,512]{1,0:T(8,128)(2,1)}, bf16[8,16,512]{2,1,0:T(8,128)(2,1)}) custom-call(bf16[256,512]{1,0:T(8,128)(2,1)} %bitcast.11, bf16[256,512]{1,0:T(8,128)(2,1)} %bitcast.12, bf16[256,512]{1,0:T(8,128)(2,1)} %bitcast.13, bf16[256,512]{1,0:T(8,128)(2,1)} %bitcast.14, bf16[256,512]{1,0:T(8,128)(2,1)} %filt_h.1, ...), custom_call_target="tpu_custom_call" | custom-call | tf_op jit(solution)/shard_map/window_backward/pallas_call | solution.py:384
  38.7 2.1 %results.1 = (bf16[256,512]{1,0:T(8,128)(2,1)}, bf16[256,512]{1,0:T(8,128)(2,1)}, bf16[256,512]{1,0:T(8,128)(2,1)}, f32[64,512]{1,0:T(8,128)}, f32[64,512]{1,0:T(8,128)}) custom-call(bf16[4,256,128]{2,1,0:T(8,128)(2,1)} %get-tuple-element.13.gm_h, bf16[256,512]{1,0:T(8,128)(2,1)} %get-tuple-element.14.gx2_h, bf16[8,16,512]{2,1,0:T(8,128)(2,1)} %get-tuple-element.15.fin_h, ...), custom_call_target="tpu_custom_call" | custom-call | tf_op jit(solution)/shard_map/results/pallas_call | solution.py:423
